TPU v7x, 32 devices: a whole 2x2x4 slice. The times are simulated.
32 devices in a mesh: tm: 8 (over z, y), pix: 4 (over x, core).
Axes of the slice: x: 2, y: 2, z: 4, core: 2. Of those that a mesh axis runs over, the one named last changes fastest.
Arguments:
- frames: bfloat16 [1024, 131072], P('tm', 'pix'), may hold values from -30 to 30, as said below
- band_edges: int32 [65], replicated, may hold values from 0 to 384, as said below
Outputs:
- coherence: float32 [64, 2, 8, 8], P('tm')
Inputs may be any that keep to these rules, and one draw needn't show every extreme that they name: `frames`: image intensities with a level of their own in each pixel. Strictly increasing, band_edges[0] = 0 and band_edges[64] = 384; the bands have uneven widths.
All inputs are finite; a program needn't handle non-finite values.
Results may differ from a plain program's by a relative error of at most 0.0096.
Values may be sent and summed in bfloat16 or wider, within the bound.
A program may use at most 192 MiB of HBM per device.

v0:
```python
import math

import jax
import jax.numpy as jnp
from jax import lax
from jax.sharding import PartitionSpec as P

TAPERS = 8
NB = 384
NBANDS = 64


def partner(value, axis, bit):
    mask = 2**bit
    pairs = [(source, source ^ mask) for source in range(lax.axis_size(axis))]
    return lax.ppermute(value, axis, pairs)


def transform_table(length, bins, tapers):
    frame_ids = jnp.arange(length, dtype=jnp.int32)
    bin_ids = jnp.arange(bins, dtype=jnp.int32)
    phase = (bin_ids[:, None] * frame_ids[None, :] % length).astype(jnp.float32) * (
        2.0 * math.pi / length
    )
    orders = jnp.arange(1, tapers + 1, dtype=jnp.int32).astype(jnp.float32)
    taper_rows = math.sqrt(2.0 / (length + 1)) * jnp.sin(
        math.pi * orders[:, None] * (frame_ids[None, :].astype(jnp.float32) + 1.0) / (length + 1)
    )
    real_part = taper_rows[:, None, :] * jnp.cos(phase)[None]
    imag_part = -taper_rows[:, None, :] * jnp.sin(phase)[None]
    dft_table = jnp.stack([real_part, imag_part], axis=1)
    return dft_table.reshape(tapers * 2 * bins, length).astype(jnp.bfloat16)


def bin_cross(spectra, tapers, bins):
    rows_by_part = spectra.reshape(2 * tapers, bins, -1)
    per_bin = jnp.einsum(
        "afp,bfp->fab", rows_by_part, rows_by_part, precision=lax.Precision.HIGHEST
    )
    return per_bin.reshape(bins, 4 * tapers * tapers)


def band_matrix(band_edges, bins):
    bin_ids = jnp.arange(bins, dtype=jnp.int32)
    band_mask = (bin_ids[None, :] >= band_edges[:-1, None]) & (
        bin_ids[None, :] < band_edges[1:, None]
    )
    return band_mask.astype(jnp.float32)


def coherence_of(band_sums, counts, total_pixels, tapers):
    blocks = band_sums.reshape(-1, tapers, 2, tapers, 2)
    real_part = blocks[:, :, 0, :, 0] + blocks[:, :, 1, :, 1]
    imag_part = blocks[:, :, 1, :, 0] - blocks[:, :, 0, :, 1]
    power_diag = jnp.diagonal(real_part, axis1=1, axis2=2) + 1e-06
    denominator = jnp.sqrt(power_diag[:, :, None] * power_diag[:, None, :])
    scaling = jnp.sqrt(counts * jnp.float32(total_pixels))[:, None, None]
    off_diagonal = 1.0 - jnp.eye(tapers, dtype=jnp.float32)
    factor = scaling * off_diagonal / denominator
    return jnp.stack([real_part * factor, imag_part * factor], axis=1)


def local(frames, band_edges):
    groups = lax.axis_size("tm")
    frames_dev, pix_dev = frames.shape
    share_cols = pix_dev // groups
    frame_total = frames_dev * groups
    dft_table = transform_table(frame_total, NB, TAPERS)
    position = lax.axis_index("tm")
    partner_order = jnp.bitwise_xor(jnp.arange(groups, dtype=jnp.int32), position)
    slot_data = frames.reshape(frames_dev, groups, share_cols).transpose(1, 0, 2)
    slot_data = jnp.take(slot_data, partner_order, axis=0)
    for level in range(groups.bit_length() - 1):
        stride = 1 << level
        halves = slot_data.reshape(groups // (2 * stride), 2, stride, frames_dev, share_cols)
        received = partner(halves[:, 1], "tm", level)
        slot_data = jnp.stack([halves[:, 0], received], axis=1).reshape(
            groups, frames_dev, share_cols
        )
    slot_data = jnp.take(slot_data, partner_order, axis=0)
    widened = slot_data.reshape(frame_total, share_cols).astype(jnp.float32)
    frame_mean = jnp.mean(widened, axis=0, keepdims=True)
    centered = (widened - frame_mean).astype(jnp.bfloat16)
    spectra = jnp.dot(dft_table, centered, preferred_element_type=jnp.float32)
    per_bin = bin_cross(spectra, TAPERS, NB)
    band_mask = band_matrix(band_edges, NB)
    partial_value = jnp.dot(band_mask, per_bin, precision=lax.Precision.HIGHEST)
    counts = jnp.sum(band_mask, axis=1)
    own_bands = NBANDS // groups
    first_band = lax.axis_index("tm") * own_bands
    total_pixels = pix_dev * lax.axis_size("pix")
    summed = lax.psum(partial_value, ("tm", "pix"))
    own_sums = lax.dynamic_slice_in_dim(summed, first_band, own_bands, 0)
    own_counts = lax.dynamic_slice_in_dim(counts, first_band, own_bands, 0)
    return coherence_of(own_sums, own_counts, total_pixels, TAPERS)


def solution(mesh):
    return jax.shard_map(
        local,
        mesh=mesh,
        in_specs=(P("tm", "pix"), P()),
        out_specs=P("tm", None, None, None),
        check_vma=False,
    )
```

profile of v0, /device:TPU:0, one launch (start us, length us, event | category | flops | bytes accessed | tf_op | source)
XLA Modules:
  0.0 800.6 jit_solution(6375300739627746019)
XLA Ops:
  6.5 0.0 all-reduce.2.cloned.1.call-start
  6.6 11.3 %copy.31 = bf16[128,32768]{0,1:T(8,128)(2,1)} copy(bf16[128,32768]{1,0:T(8,128)(2,1)} %param.4) | data formatting | bytes 16777216 | tf_op args[0]
  17.9 11.5 %copy.32 = bf16[128,8,4096]{2,0,1:T(8,128)(2,1)} copy(bf16[128,8,4096]{0,2,1:T(8,128)(2,1)} %bitcast.49) | data formatting | bytes 16777216 | tf_op jit(solution)/shard_map/reshape | solution.py:71
  29.4 8.1 %gather_fusion.1 = bf16[8,128,4096]{2,1,0:T(8,128)(2,1)} fusion(bf16[8,128,4096]{2,1,0:T(8,128)(2,1)} %bitcast.47, s32[1024]{0:T(1024)S(1)} %pad_clamp_fusion), kind=kCustom, calls=%fused_computation.clone | custom fusion | bytes 16777248 | tf_op jit(solution)/shard_map/jit(_take)/gather | solution.py:72
  37.5 7.5 broadcast_select_fusion
  45.0 4.0 fusion.18
  48.9 3.0 collective-permute-start
  52.0 90.6 %collective-permute-done = bf16[4,1,128,4096]{3,2,0,1:T(8,128)(2,1)S(1)} collective-permute-done((bf16[4,1,128,4096]{3,2,0,1:T(8,128)(2,1)S(1)}, bf16[4,1,128,4096]{3,2,0,1:T(8,128)(2,1)S(1)}, u32[]{:S(2)}, u32[]{:S(2)}) %collective-permute-start) | collective-permute-done | bytes 4194336 | tf_op jit(solution)/shard_map/ppermute | solution.py:16
  142.5 0.7 fusion.1
  143.3 1.9 collective-permute-start.1
  145.2 5.7 fusion.10
  150.8 6.6 fusion.9
  157.4 0.2 sine_multiply_fusion
  157.6 77.5 %collective-permute-done.1 = bf16[2,2,128,4096]{3,2,0,1:T(8,128)(2,1)S(1)} collective-permute-done((bf16[2,2,128,4096]{3,2,0,1:T(8,128)(2,1)S(1)}, bf16[2,2,128,4096]{3,2,0,1:T(8,128)(2,1)S(1)}, u32[]{:S(2)}, u32[]{:S(2)}) %collective-permute-start.1) | collective-permute-done | bytes 4194336 | tf_op jit(solution)/shard_map/ppermute | solution.py:16
  235.1 0.0 copy-start.1
  235.1 1.9 copy-done.1
  237.1 6.2 pad_maximum_fusion.1
  243.3 7.7 copy.37
  251.0 0.0 copy-start
  251.0 6.0 fusion.17
  257.0 2.5 collective-permute-start.2
  259.5 0.0 copy-done
  259.5 18.9 %multiply_convert_fusion = (bf16[8,1,384,1024]{3,1,0,2:T(2,128)(2,1)S(1)}, bf16[8,1,384,1024]{3,1,0,2:T(2,128)(2,1)}) fusion(f32[384,1024]{1,0:T(8,128)S(1)} %copy-done, f32[8,1024]{1,0:T(8,128)S(1)} %get-tuple-element.19, f32[384,1024]{1,0:T(8,128)S(1)} %fusion.10, f32[8,1024]{1,0:T(8,128)S(1)} %get-tuple-element.18), kind=kLoop, calls=%fused_computation.7 | loop fusion | flops 12582912 | bytes 15794176 | tf_op jit(solution)/shard_map/convert.1
  278.4 31.0 %pad_maximum_fusion = bf16[8,2,384,1024]{3,1,0,2:T(2,128)(2,1)} fusion(bf16[8,1,384,1024]{3,1,0,2:T(2,128)(2,1)S(1)} %get-tuple-element.22, bf16[8,1,384,1024]{3,1,0,2:T(2,128)(2,1)} %get-tuple-element.23), kind=kLoop, calls=%fused_computation.6 | loop fusion | flops 25165824 | bytes 25165824 | tf_op jit(solution)/shard_map/stack | solution.py:31
  309.4 0.0 copy-start.8
  309.4 19.1 %convert_element_type.66 = bf16[16,384,1024]{2,0,1:T(8,128)(2,1)} reshape(bf16[8,2,384,1024]{3,1,0,2:T(2,128)(2,1)} %pad_maximum_fusion) | data formatting | bytes 25165824 | tf_op jit(solution)/shard_map/convert_element_type | solution.py:32
  328.4 0.5 or_bitcast_fusion
  329.0 0.6 convert_subtract_fusion.1
  329.5 0.0 copy-done.8
  329.5 0.1 fusion.20
  329.6 0.0 copy-start.4
  329.6 0.0 copy-start.6
  329.6 0.5 copy-done.4
  330.1 0.7 convert_reduce_fusion.1
  330.9 0.0 copy-done.6
  330.9 108.1 %collective-permute-done.2 = bf16[1,4,128,4096]{3,2,1,0:T(8,128)(2,1)} collective-permute-done((bf16[1,4,128,4096]{3,2,1,0:T(8,128)(2,1)}, bf16[1,4,128,4096]{3,2,1,0:T(8,128)(2,1)}, u32[]{:S(2)}, u32[]{:S(2)}) %collective-permute-start.2) | collective-permute-done | bytes 4194336 | tf_op jit(solution)/shard_map/ppermute | solution.py:16
  438.9 7.5 pad_maximum_fusion.2
  446.4 8.1 %gather_fusion.2 = bf16[8,128,4096]{2,1,0:T(8,128)(2,1)} fusion(bf16[8,128,4096]{2,1,0:T(8,128)(2,1)} %bitcast.46, s32[1024]{0:T(1024)S(1)} %pad_clamp_fusion), kind=kCustom, calls=%fused_computation.1.clone | custom fusion | bytes 16777248 | tf_op jit(solution)/shard_map/jit(_take)/gather | solution.py:80
  454.5 5.2 convert_reduce_fusion
  459.7 9.4 %fusion = bf16[8,128,4096]{2,1,0:T(8,128)(2,1)} fusion(f32[4096]{0:T(1024)S(1)} %broadcast_multiply_fusion, bf16[8,128,4096]{2,1,0:T(8,128)(2,1)} %gather_fusion.2, pred[8]{0:T(512)(128)(4,1)S(1)} %compare_and_fusion), kind=kLoop, calls=%fused_computation.5 | loop fusion | flops 16777216 | bytes 16793608 | tf_op jit(solution)/shard_map/convert_element_type | solution.py:83
  469.1 61.8 %fusion.21 = f32[16,384,4096]{2,0,1:T(8,128)} fusion(bf16[16,384,1024]{2,0,1:T(8,128)(2,1)} %convert_element_type.66, bf16[1024,4096,1]{1,0,2:T(8,128)(2,1)} %bitcast.51), kind=kOutput, calls=%fused_computation.61 | convolution fusion | flops 51539607552 | bytes 121634816 | tf_op jit(solution)/shard_map/dot_general | solution.py:84
  530.9 0.0 copy-start.5
  530.9 0.0 copy-start.7
  530.9 0.0 copy-start.2
  531.0 0.0 copy-start.3
  531.0 139.9 %fusion.22 = f32[384,16,16]{2,1,0:T(8,128)S(1)} fusion(f32[16,384,4096]{2,0,1:T(8,128)} %fusion.21), kind=kOutput, calls=%fused_computation.62 | convolution fusion | flops 4831838208 | bytes 101056512 | tf_op jit(solution)/shard_map/afp,bfp->fab/dot_general | solution.py:37
  670.9 1.1 copy.38
  672.0 0.0 copy-done.5
  672.0 0.0 copy-done.7
  672.0 1.0 fusion.12
  673.0 0.0 all-reduce.2.cloned.1.call-update
  673.0 0.7 multiply_sqrt_fusion
  673.7 117.7 %all-reduce.2.cloned.1.call-done = f32[64,256]{1,0:T(8,128)} async-done(((f32[64,256]{1,0:T(8,128)}), f32[64,256]{1,0:T(8,128)}) %all-reduce.2.cloned.1.call-update) | async-done | bytes 65552 | tf_op jit(solution)/shard_map/psum | solution.py:92
  791.4 0.7 constant_dynamic-slice_fusion
  792.1 0.1 copy.39
  792.2 0.1 fusion.19
  792.4 0.0 copy-done.2
  792.4 0.6 gather_fusion
  792.9 0.0 copy-done.3
  793.0 0.1 bitcast_multiply_fusion.1
  793.1 0.7 copy.44
  (9 shorter events, 0.1 us)
Async XLA Ops:
  6.5 784.9 %all-reduce.2.cloned.1.call-start = ((), (), s32[]{:S(2)}) async-start(), calls=%async_computation | async-start | bytes 131072 | tf_op jit(solution)/shard_map/psum | solution.py:92
  48.9 93.6 %collective-permute-start = (bf16[4,1,128,4096]{3,2,0,1:T(8,128)(2,1)S(1)}, bf16[4,1,128,4096]{3,2,0,1:T(8,128)(2,1)S(1)}, u32[]{:S(2)}, u32[]{:S(2)}) collective-permute-start(bf16[4,1,128,4096]{3,2,0,1:T(8,128)(2,1)S(1)} %get-tuple-element.11), channel_id=1, source_target_pairs={{0,4},{4,0},{8,12},{12,8},{16,20},{20,16},{24,28},{28,24},{1,5},{5... | collective-permute-start | bytes 12582920 | tf_op jit(solution)/shard_map/ppermute | solution.py:16
  143.3 91.8 %collective-permute-start.1 = (bf16[2,2,128,4096]{3,2,0,1:T(8,128)(2,1)S(1)}, bf16[2,2,128,4096]{3,2,0,1:T(8,128)(2,1)S(1)}, u32[]{:S(2)}, u32[]{:S(2)}) collective-permute-start(bf16[2,2,128,4096]{3,2,0,1:T(8,128)(2,1)S(1)} %get-tuple-element.9), channel_id=1, source_target_pairs={{0,8},{4,12},{8,0},{12,4},{16,24},{20,28},{24,16},{28,20},{1,9},{5... | collective-permute-start | bytes 12582920 | tf_op jit(solution)/shard_map/ppermute | solution.py:16
  235.1 1.9 copy-start.1
  251.0 8.5 %copy-start = (f32[384,1024]{1,0:T(8,128)S(1)}, f32[384,1024]{1,0:T(8,128)}, u32[]{:S(2)}) copy-start(f32[384,1024]{1,0:T(8,128)} %fusion.9) | copy-start | bytes 4718596
  257.0 181.9 %collective-permute-start.2 = (bf16[1,4,128,4096]{3,2,1,0:T(8,128)(2,1)}, bf16[1,4,128,4096]{3,2,1,0:T(8,128)(2,1)}, u32[]{:S(2)}, u32[]{:S(2)}) collective-permute-start(bf16[1,4,128,4096]{3,2,1,0:T(8,128)(2,1)} %get-tuple-element.7), channel_id=1, source_target_pairs={{0,16},{4,20},{8,24},{12,28},{16,0},{20,4},{24,8},{28,12},{1,17},{... | collective-permute-start | bytes 12582920 | tf_op jit(solution)/shard_map/ppermute | solution.py:16
  309.4 20.2 %copy-start.8 = (s32[65]{0:T(128)S(1)}, s32[65]{0:T(128)}, u32[]{:S(2)}) copy-start(s32[65]{0:T(128)} %param.5) | copy-start | bytes 784
  329.6 0.5 copy-start.4
  329.6 1.2 copy-start.6
  530.9 141.0 %copy-start.5 = (s32[64]{0:T(128)S(1)}, s32[64]{0:T(128)}, u32[]{:S(2)}) copy-start(s32[64]{0:T(128)} %copy-done.4) | copy-start | bytes 772
  530.9 141.0 %copy-start.7 = (s32[64]{0:T(128)S(1)}, s32[64]{0:T(128)}, u32[]{:S(2)}) copy-start(s32[64]{0:T(128)} %copy-done.6) | copy-start | bytes 772
  530.9 261.4 %copy-start.2 = (s32[8]{0:T(128)S(1)}, s32[8]{0:T(128)}, u32[]{:S(2)}) copy-start(s32[8]{0:T(128)} %or_bitcast_fusion) | copy-start | bytes 100
  531.0 262.0 %copy-start.3 = (f32[8,8]{1,0:T(8,128)S(1)}, f32[8,8]{1,0:T(8,128)}, u32[]{:S(2)}) copy-start(f32[8,8]{1,0:T(8,128)} %convert_subtract_fusion.1) | copy-start | bytes 772
Sparse Core Ops, SparseCore 0:
  673.1 118.2 all-reduce.1
where the time goes:
time: 803 us; the launch traced here: 801 us
  waiting for transfers between devices  394 us (49%)
  matrix products  203 us (25%)
  other arithmetic  101 us (13%)
  local copies, waits for them, and re-layouts  81.6 us (10%)
  between operations  13.5 us (2%)
    ppermute x3, waiting for transfers between devices, partner(): return lax.ppermute(value, axis, pairs)  276 us
    dot_general x1, matrix products, bin_cross(): jnp.einsum('afp,bfp->fab', rows_by_part, rows_by_part, precision=lax.Prec...  140 us
    psum x1, waiting for transfers between devices, local(): summed = lax.psum(partial_value, ('tm', 'pix'))  118 us
    dot_general x1, matrix products, local(): spectra = jnp.dot(dft_table, centered, preferred_element_type=jnp.float32)  61.8 us
    another operation x1, other arithmetic, transform_table(): dft_table = jnp.stack([real_part, imag_part], axis=1)  31 us
    convert_element_type x1, local copies, waits for them, and re-layouts, transform_table(): return dft_table.reshape(tapers * 2 * bins, length).astype(jnp.bfloat16)  19.1 us
    another operation x1, other arithmetic  18.9 us
    gather x2, local copies, waits for them, and re-layouts, local(): slot_data = jnp.take(slot_data, partner_order, axis=0)  16.1 us
  transfers between devices with their start and end apart: 4, of which 4 were waited for; matrix products, arithmetic and copies ran while one was open for 10% of the time, Pallas kernels for 0%

commit v1 on v0

v1 whole, which is shorter than its diff:
```python
import functools
import math

import jax
import jax.numpy as jnp
import ml_dtypes
import numpy as np
from jax import lax
from jax.experimental import pallas as pl
from jax.experimental.pallas import tpu as pltpu
from jax.sharding import PartitionSpec as P

TAPERS = 8
NB = 384
NBANDS = 64
PAIRS = TAPERS * TAPERS
BINS = 8
TILE = 256
CHUNK = 256
GROUP = 2 * TAPERS * BINS
GROUPS = NB // BINS
ROWS = 1024
MESH = pl.DeviceIdType.MESH
HIGHEST = lax.Precision.HIGHEST


def tables(length):
    frames = np.arange(length)
    phase = (np.arange(NB)[:, None] * frames[None, :] % length) * (2.0 * math.pi / length)
    trig = np.stack([np.cos(phase), -np.sin(phase)]).reshape(2, GROUPS, BINS, length)
    trig = trig.transpose(1, 0, 2, 3).reshape(2 * NB, length).astype(np.float32)
    rate = np.pi * (np.arange(TAPERS) + 1.0) / (length + 1)
    tapers = math.sqrt(2.0 / (length + 1)) * np.sin(rate[:, None] * (frames + 1.0))
    combine = np.zeros((2 * TAPERS, 2 * TAPERS, BINS, 2 * PAIRS), np.float32)
    power = np.zeros((2 * PAIRS, 2, 2, TAPERS, TAPERS), np.float32)
    for k in range(TAPERS):
        for l in range(TAPERS):
            kl = k * TAPERS + l
            combine[2 * k, 2 * l, :, kl] = 1.0
            combine[2 * k + 1, 2 * l + 1, :, kl] = 1.0
            combine[2 * k + 1, 2 * l, :, PAIRS + kl] = 1.0
            combine[2 * k, 2 * l + 1, :, PAIRS + kl] = -1.0
            power[k * TAPERS + k, 0, :, k, l] = 1.0
            power[l * TAPERS + l, 1, :, k, l] = 1.0
    combine = combine.reshape(2 * TAPERS * GROUP, 2 * PAIRS).astype(ml_dtypes.bfloat16)
    return trig, tapers.astype(np.float32), combine, power.reshape(2 * PAIRS, 4 * PAIRS)


def split(value):
    high = value.astype(jnp.bfloat16)
    return high, (value - high.astype(jnp.float32)).astype(jnp.bfloat16)


def kernel(
    groups, pixes, total_pixels,
    edges_ref, frames_ref, trig_hbm, tapers_hbm, combine_hbm, power_hbm,
    out_ref,
    data, centered, table, cross, trig, tapers, combine, power, mask, counts,
    part, got_tm, share, got_pix,
    table_sem, local_sem, send_sem, recv_sem, send_tm, recv_tm, send_pix, recv_pix,
):
    me = lax.axis_index("tm")
    me_pix = lax.axis_index("pix")
    chunks, frame_total, cols = data.shape
    frames_dev = frame_total // groups
    share_cols = chunks * cols
    own_bands = NBANDS // groups
    tiles = frame_total // TILE
    steps = sorted(range(1, groups), key=lambda d: (abs(d - groups // 2), d))

    def rows_of(group):
        return pl.ds(pl.multiple_of(group * frames_dev, frames_dev), frames_dev)

    def columns_of(group, s):
        return pl.ds(pl.multiple_of(group * share_cols + s * cols, 128), cols)

    barrier = pltpu.get_barrier_semaphore()
    for d in range(1, groups):
        pl.semaphore_signal(
            barrier, inc=1, device_id=(lax.rem(me + d, groups), me_pix), device_id_type=MESH
        )
    for d in range(1, pixes):
        pl.semaphore_signal(
            barrier, inc=1, device_id=(me, lax.rem(me_pix + d, pixes)), device_id_type=MESH
        )
    pl.semaphore_wait(barrier, groups - 1 + pixes - 1)

    def frame_copy(s, d):
        to = lax.rem(me + d, groups)
        return pltpu.make_async_remote_copy(
            src_ref=frames_ref.at[:, columns_of(to, s)],
            dst_ref=data.at[s, rows_of(me), :],
            send_sem=send_sem.at[s, d],
            recv_sem=recv_sem.at[s, d],
            device_id=(to, me_pix),
            device_id_type=MESH,
        )

    def own_copy(s):
        return pltpu.make_async_copy(
            frames_ref.at[:, columns_of(me, s)], data.at[s, rows_of(me), :], local_sem.at[s]
        )

    def send(s, carry):
        for d in steps:
            frame_copy(s, d).start()
        own_copy(s).start()
        return carry

    lax.fori_loop(0, chunks, send, 0)

    table_copies = [
        pltpu.make_async_copy(source, target, table_sem.at[i])
        for i, (source, target) in enumerate(
            [(trig_hbm, trig), (tapers_hbm, tapers), (combine_hbm, combine), (power_hbm, power)]
        )
    ]
    for copy in table_copies:
        copy.start()

    bin_ids = lax.broadcasted_iota(jnp.int32, (1, NB), 1)
    for b in range(NBANDS):
        inside = (bin_ids >= edges_ref[b]) & (bin_ids < edges_ref[b + 1])
        mask[b:b + 1, :] = jnp.where(inside, 1.0, 0.0)
        count = (edges_ref[b + 1] - edges_ref[b]).astype(jnp.float32)
        counts[b // own_bands, b % own_bands:b % own_bands + 1, :] = jnp.full(
            (1, 2 * PAIRS), count, jnp.float32
        )
    for copy in table_copies:
        copy.wait()
    cross[...] = jnp.zeros_like(cross)

    def fill(g, carry):
        waves = trig[pl.ds(pl.multiple_of(g * 2 * BINS, 2 * BINS), 2 * BINS), :]
        for k in range(TAPERS):
            rows = pl.ds(pl.multiple_of(g * GROUP + k * 2 * BINS, 2 * BINS), 2 * BINS)
            table[rows, :] = (waves * tapers[k:k + 1, :]).astype(jnp.bfloat16)
        return carry

    lax.fori_loop(0, GROUPS, fill, 0)

    def accumulate(s, carry):
        own_copy(s).wait()
        for d in steps:
            source = lax.rem(me + groups - d, groups)
            pltpu.make_async_remote_copy(
                src_ref=frames_ref.at[:, columns_of(me, s)],
                dst_ref=data.at[s, rows_of(source), :],
                send_sem=send_sem.at[s, d],
                recv_sem=recv_sem.at[s, d],
                device_id=(source, me_pix),
                device_id_type=MESH,
            ).wait_recv()
        total = jnp.zeros((1, cols), jnp.float32)
        for i in range(tiles):
            block = data[s, i * TILE:(i + 1) * TILE, :].astype(jnp.float32)
            total = total + jnp.sum(block, axis=0, keepdims=True)
        mean = total * (1.0 / frame_total)
        for i in range(tiles):
            block = data[s, i * TILE:(i + 1) * TILE, :].astype(jnp.float32)
            block = (block - mean).astype(jnp.bfloat16)
            centered[i * TILE:(i + 1) * TILE, :] = block

        def transform(r, inner):
            rows = pl.ds(pl.multiple_of(r * ROWS, ROWS), ROWS)
            spectra = jnp.dot(
                table[rows, :], centered[...], preferred_element_type=jnp.float32
            ).astype(jnp.bfloat16)
            for g in range(ROWS // GROUP):
                block = spectra[g * GROUP:(g + 1) * GROUP]
                cross[r * (ROWS // GROUP) + g] += lax.dot_general(
                    block, block, (((1,), (1,)), ((), ())), preferred_element_type=jnp.float32
                )
            return inner

        return lax.fori_loop(0, GROUPS * GROUP // ROWS, transform, carry)

    lax.fori_loop(0, chunks, accumulate, 0)

    band_mask = mask[...].astype(jnp.bfloat16)
    same_bin = (
        lax.broadcasted_iota(jnp.int32, (BINS, GROUP), 1) % BINS
        == lax.broadcasted_iota(jnp.int32, (BINS, GROUP), 0)
    )
    pieces = []
    for a in range(0, 2 * TAPERS, 2):
        sides = []
        for row in (a, a + 1):
            side = jnp.where(same_bin[None], cross[:, row * BINS:(row + 1) * BINS, :], 0.0)
            sides.append(side.reshape(NB, GROUP))
        high, low = split(jnp.concatenate(sides, axis=1))
        pieces.append(
            jnp.dot(band_mask, high, preferred_element_type=jnp.float32)
            + jnp.dot(band_mask, low, preferred_element_type=jnp.float32)
        )
    high, low = split(jnp.concatenate(pieces, axis=1))
    both = jnp.dot(
        jnp.concatenate([high, low], axis=0), combine[...], preferred_element_type=jnp.float32
    )
    both = both[:NBANDS] + both[NBANDS:]
    for g in range(groups):
        part[g] = both[g * own_bands:(g + 1) * own_bands, :]

    def band_copy(d, target, slot):
        return pltpu.make_async_remote_copy(
            src_ref=part.at[target],
            dst_ref=got_tm.at[slot],
            send_sem=send_tm.at[d],
            recv_sem=recv_tm.at[d],
            device_id=(target, me_pix),
            device_id_type=MESH,
        )

    for d in steps:
        band_copy(d, lax.rem(me + d, groups), me).start()
    got_tm[me] = part[me]
    for d in steps:
        source = lax.rem(me + groups - d, groups)
        band_copy(d, source, source).wait_recv()
    value = got_tm[0]
    for g in range(1, groups):
        value = value + got_tm[g]
    share[...] = value
    got_pix[me_pix] = value

    def share_copy(d, target, slot):
        return pltpu.make_async_remote_copy(
            src_ref=share,
            dst_ref=got_pix.at[slot],
            send_sem=send_pix.at[d],
            recv_sem=recv_pix.at[d],
            device_id=(me, target),
            device_id_type=MESH,
        )

    for d in range(1, pixes):
        share_copy(d, lax.rem(me_pix + d, pixes), me_pix).start()
    for d in range(1, pixes):
        source = lax.rem(me_pix + pixes - d, pixes)
        share_copy(d, source, source).wait_recv()
    value = got_pix[0]
    for g in range(1, pixes):
        value = value + got_pix[g]

    powers = jnp.dot(value, power[...], precision=HIGHEST, preferred_element_type=jnp.float32)
    power_k = powers[:, :2 * PAIRS] + 1e-6
    power_l = powers[:, 2 * PAIRS:] + 1e-6
    lane = lax.broadcasted_iota(jnp.int32, value.shape, 1) % PAIRS
    off_diagonal = jnp.where(lane // TAPERS == lane % TAPERS, 0.0, 1.0)
    scaling = jnp.sqrt(counts[me] * total_pixels)
    out_ref[...] = value * (scaling * off_diagonal / jnp.sqrt(power_k * power_l))

    def drain(s, carry):
        for d in steps:
            frame_copy(s, d).wait_send()
        return carry

    lax.fori_loop(0, chunks, drain, 0)
    for d in steps:
        band_copy(d, lax.rem(me + d, groups), me).wait_send()
    for d in range(1, pixes):
        share_copy(d, lax.rem(me_pix + d, pixes), me_pix).wait_send()


def local(frames, band_edges):
    groups = lax.axis_size("tm")
    pixes = lax.axis_size("pix")
    frames_dev, pix_dev = frames.shape
    frame_total = frames_dev * groups
    share_cols = pix_dev // groups
    cols = min(CHUNK, share_cols)
    chunks = share_cols // cols
    own_bands = NBANDS // groups
    trig, tapers, combine, power = tables(frame_total)
    anywhere = pl.BlockSpec(memory_space=pl.ANY)
    lanes = 2 * PAIRS
    result = pl.pallas_call(
        functools.partial(kernel, groups, pixes, float(pix_dev * pixes)),
        out_shape=jax.ShapeDtypeStruct((own_bands, lanes), jnp.float32),
        in_specs=[pl.BlockSpec(memory_space=pltpu.SMEM)] + [anywhere] * 5,
        out_specs=pl.BlockSpec(memory_space=pltpu.VMEM),
        scratch_shapes=[
            pltpu.VMEM((chunks, frame_total, cols), jnp.bfloat16),
            pltpu.VMEM((frame_total, cols), jnp.bfloat16),
            pltpu.VMEM((GROUPS * GROUP, frame_total), jnp.bfloat16),
            pltpu.VMEM((GROUPS, GROUP, GROUP), jnp.float32),
            pltpu.VMEM(trig.shape, jnp.float32),
            pltpu.VMEM(tapers.shape, jnp.float32),
            pltpu.VMEM(combine.shape, jnp.bfloat16),
            pltpu.VMEM(power.shape, jnp.float32),
            pltpu.VMEM((NBANDS, NB), jnp.float32),
            pltpu.VMEM((groups, own_bands, lanes), jnp.float32),
            pltpu.VMEM((groups, own_bands, lanes), jnp.float32),
            pltpu.VMEM((groups, own_bands, lanes), jnp.float32),
            pltpu.VMEM((own_bands, lanes), jnp.float32),
            pltpu.VMEM((pixes, own_bands, lanes), jnp.float32),
            pltpu.SemaphoreType.DMA((4,)),
            pltpu.SemaphoreType.DMA((chunks,)),
            pltpu.SemaphoreType.DMA((chunks, groups)),
            pltpu.SemaphoreType.DMA((chunks, groups)),
            pltpu.SemaphoreType.DMA((groups,)),
            pltpu.SemaphoreType.DMA((groups,)),
            pltpu.SemaphoreType.DMA((pixes,)),
            pltpu.SemaphoreType.DMA((pixes,)),
        ],
        compiler_params=pltpu.CompilerParams(
            collective_id=0, has_side_effects=True, vmem_limit_bytes=56 * 2**20
        ),
        cost_estimate=pl.CostEstimate(
            flops=2 * GROUPS * GROUP * frame_total * share_cols,
            bytes_accessed=4 * frame_total * share_cols,
            transcendentals=0,
        ),
        name="band_coherence",
    )(band_edges, frames, trig, tapers, combine, power)
    return result.reshape(own_bands, 2, TAPERS, TAPERS)


def solution(mesh):
    return jax.shard_map(
        local,
        mesh=mesh,
        in_specs=(P("tm", "pix"), P()),
        out_specs=P("tm", None, None, None),
        check_vma=False,
    )
```

time: 803 us -> 212 us (0.26)
  waiting for transfers between devices: 394 us -> 0 us
  Pallas kernels: 0 us -> 210 us
  matrix products: 203 us -> 0 us
  other arithmetic: 101 us -> 0 us
  local copies, waits for them, and re-layouts: 81.6 us -> 1.4 us
  between operations: 13.5 us -> 0.01 us
    ppermute x3 -> x0, waiting for transfers between devices: 276 us -> none  [partner(): return lax.ppermute(value, axis, pairs)]
    pallas_call x0 -> x1, Pallas kernels: none -> 210 us  [local(): pl.pallas_call(functools.partial(kernel, groups, pixes, float(pix_dev * p...]
    dot_general x3 -> x0, matrix products: 203 us -> none  [the longest x1 140 us: bin_cross(): jnp.einsum('afp,bfp->fab', rows_by_part, rows_by_part, precision=lax.Prec...]
    psum x1 -> x0, waiting for transfers between devices: 118 us -> none  [local(): summed = lax.psum(partial_value, ('tm', 'pix'))]
    another operation x6 -> x0, other arithmetic: 64.3 us -> none  [the longest x1 31 us: transform_table(): dft_table = jnp.stack([real_part, imag_part], axis=1)]
    convert_element_type x1 -> x0, local copies, waits for them, and re-layouts: 19.1 us -> none  [transform_table(): return dft_table.reshape(tapers * 2 * bins, length).astype(jnp.bfloat16)]
    gather x3 -> x0, local copies, waits for them, and re-layouts: 16.7 us -> none  [the longest x2 16.1 us: local(): slot_data = jnp.take(slot_data, partner_order, axis=0)]
    unnamed x19 -> x0, local copies, waits for them, and re-layouts: 13.8 us -> none
  transfers between devices with their start and end apart: 4 -> 0, of which waited for: 4 -> 0; matrix products, arithmetic and copies ran while one was open for 10% -> 0% of each run, Pallas kernels for 0% -> 0%
where the time goes in v1:
time: 212 us
  Pallas kernels  210 us (99%)
    pallas_call x1, Pallas kernels, local(): pl.pallas_call(functools.partial(kernel, groups, pixes, float(pix_dev * p...  210 us

profile of v1, /device:TPU:0, one launch (start us, length us, event | category | flops | bytes accessed | tf_op | source)
XLA Modules:
  0.0 211.8 jit_solution(6454406223500247821)
XLA Ops:
  0.0 210.4 %band_coherence.1 = f32[8,128]{1,0:T(8,128)} custom-call(s32[65]{0:T(128)} %edges_ref.1, bf16[128,32768]{1,0:T(8,128)(2,1)} %frames_ref.1, f32[768,1024]{1,0:T(8,128)} %constant.8.clone.trig_hbm, f32[8,1024]{1,0:T(8,128)} %constant.9.clone.tapers_hbm, bf16[2048,128]{1,0:T(8,128)(2,1)} %constant.10.clone.combine_hbm, f32[128,256]{1,0:T(8,128)} %constant.11.clone.power_hbm), custom_call_target="tpu_custom_call" | custom-call | flops 51539607552 | bytes 16777216 | tf_op jit(solution)/shard_map/band_coherence/pallas_call | solution.py:277
  210.4 1.4 reshape.3

commit v2 on v1

--- a/solution.py
+++ b/solution.py
@@ -66,7 +66,18 @@
     share_cols = chunks * cols
     own_bands = NBANDS // groups
     tiles = frame_total // TILE
-    steps = sorted(range(1, groups), key=lambda d: (abs(d - groups // 2), d))
+    half = groups // 2
+    base = me // half * half
+    mine = me - base
+    across = list(range(half))
+    beside = list(range(half + 1, groups))
+    peers = across + beside
+
+    def target_of(d):
+        return (half - base if d < half else base) + lax.rem(mine + d, half)
+
+    def source_of(d):
+        return (half - base if d < half else base) + lax.rem(mine + groups - d, half)
 
     def rows_of(group):
         return pl.ds(pl.multiple_of(group * frames_dev, frames_dev), frames_dev)
@@ -75,9 +86,9 @@
         return pl.ds(pl.multiple_of(group * share_cols + s * cols, 128), cols)
 
     barrier = pltpu.get_barrier_semaphore()
-    for d in range(1, groups):
+    for d in peers:
         pl.semaphore_signal(
-            barrier, inc=1, device_id=(lax.rem(me + d, groups), me_pix), device_id_type=MESH
+            barrier, inc=1, device_id=(target_of(d), me_pix), device_id_type=MESH
         )
     for d in range(1, pixes):
         pl.semaphore_signal(
@@ -86,7 +97,7 @@
     pl.semaphore_wait(barrier, groups - 1 + pixes - 1)
 
     def frame_copy(s, d):
-        to = lax.rem(me + d, groups)
+        to = target_of(d)
         return pltpu.make_async_remote_copy(
             src_ref=frames_ref.at[:, columns_of(to, s)],
             dst_ref=data.at[s, rows_of(me), :],
@@ -102,12 +113,21 @@
         )
 
     def send(s, carry):
-        for d in steps:
+        for d in across:
             frame_copy(s, d).start()
-        own_copy(s).start()
+        for near in (2 * s, 2 * s + 1):
+            for d in beside:
+                frame_copy(near, d).start()
+            own_copy(near).start()
         return carry
 
-    lax.fori_loop(0, chunks, send, 0)
+    def send_across(s, carry):
+        for d in across:
+            frame_copy(s, d).start()
+        return carry
+
+    lax.fori_loop(0, chunks // 2, send, 0)
+    lax.fori_loop(chunks // 2, chunks, send_across, 0)
 
     table_copies = [
         pltpu.make_async_copy(source, target, table_sem.at[i])
@@ -141,8 +161,8 @@
 
     def accumulate(s, carry):
         own_copy(s).wait()
-        for d in steps:
-            source = lax.rem(me + groups - d, groups)
+        for d in peers:
+            source = source_of(d)
             pltpu.make_async_remote_copy(
                 src_ref=frames_ref.at[:, columns_of(me, s)],
                 dst_ref=data.at[s, rows_of(source), :],
@@ -211,11 +231,11 @@
             device_id_type=MESH,
         )
 
-    for d in steps:
-        band_copy(d, lax.rem(me + d, groups), me).start()
+    for d in peers:
+        band_copy(d, target_of(d), me).start()
     got_tm[me] = part[me]
-    for d in steps:
-        source = lax.rem(me + groups - d, groups)
+    for d in peers:
+        source = source_of(d)
         band_copy(d, source, source).wait_recv()
     value = got_tm[0]
     for g in range(1, groups):
@@ -251,13 +271,13 @@
     out_ref[...] = value * (scaling * off_diagonal / jnp.sqrt(power_k * power_l))
 
     def drain(s, carry):
-        for d in steps:
+        for d in peers:
             frame_copy(s, d).wait_send()
         return carry
 
     lax.fori_loop(0, chunks, drain, 0)
-    for d in steps:
-        band_copy(d, lax.rem(me + d, groups), me).wait_send()
+    for d in peers:
+        band_copy(d, target_of(d), me).wait_send()
     for d in range(1, pixes):
         share_copy(d, lax.rem(me_pix + d, pixes), me_pix).wait_send()
 

time: 212 us -> 213 us (level)
  no operation moved by 1% of the time
where the time goes in v2:
time: 213 us; the launch traced here: 212 us
  Pallas kernels  211 us (99%)
    pallas_call x1, Pallas kernels, local(): pl.pallas_call(functools.partial(kernel, groups, pixes, float(pix_dev * p...  211 us

profile of v2, /device:TPU:0, one launch (start us, length us, event | category | flops | bytes accessed | tf_op | source)
XLA Modules:
  0.0 212.3 jit_solution(6661543736078490329)
XLA Ops:
  0.0 210.9 %band_coherence.1 = f32[8,128]{1,0:T(8,128)} custom-call(s32[65]{0:T(128)} %edges_ref.1, bf16[128,32768]{1,0:T(8,128)(2,1)} %frames_ref.1, f32[768,1024]{1,0:T(8,128)} %constant.8.clone.trig_hbm, f32[8,1024]{1,0:T(8,128)} %constant.9.clone.tapers_hbm, bf16[2048,128]{1,0:T(8,128)(2,1)} %constant.10.clone.combine_hbm, f32[128,256]{1,0:T(8,128)} %constant.11.clone.power_hbm), custom_call_target="tpu_custom_call" | custom-call | flops 51539607552 | bytes 16777216 | tf_op jit(solution)/shard_map/band_coherence/pallas_call | solution.py:297
  211.0 1.4 reshape.3

commit v3 on v2

--- a/solution.py
+++ b/solution.py
@@ -19,7 +19,7 @@
 CHUNK = 256
 GROUP = 2 * TAPERS * BINS
 GROUPS = NB // BINS
-ROWS = 1024
+ROWS = 2048
 MESH = pl.DeviceIdType.MESH
 HIGHEST = lax.Precision.HIGHEST
 
@@ -159,7 +159,7 @@
 
     lax.fori_loop(0, GROUPS, fill, 0)
 
-    def accumulate(s, carry):
+    def center(s, slot):
         own_copy(s).wait()
         for d in peers:
             source = source_of(d)
@@ -179,23 +179,40 @@
         for i in range(tiles):
             block = data[s, i * TILE:(i + 1) * TILE, :].astype(jnp.float32)
             block = (block - mean).astype(jnp.bfloat16)
-            centered[i * TILE:(i + 1) * TILE, :] = block
-
-        def transform(r, inner):
+            centered[i * TILE:(i + 1) * TILE, slot * cols:(slot + 1) * cols] = block
+
+    def accumulate(width):
+        def transform(r, carry):
             rows = pl.ds(pl.multiple_of(r * ROWS, ROWS), ROWS)
             spectra = jnp.dot(
-                table[rows, :], centered[...], preferred_element_type=jnp.float32
+                table[rows, :], centered[:, :width], preferred_element_type=jnp.float32
             ).astype(jnp.bfloat16)
-            for g in range(ROWS // GROUP):
-                block = spectra[g * GROUP:(g + 1) * GROUP]
-                cross[r * (ROWS // GROUP) + g] += lax.dot_general(
+            for g in range(ROWS // GROUP // 2):
+                block = spectra[2 * g * GROUP:2 * (g + 1) * GROUP]
+                product = lax.dot_general(
                     block, block, (((1,), (1,)), ((), ())), preferred_element_type=jnp.float32
                 )
-            return inner
-
-        return lax.fori_loop(0, GROUPS * GROUP // ROWS, transform, carry)
-
-    lax.fori_loop(0, chunks, accumulate, 0)
+                first = r * (ROWS // GROUP) + 2 * g
+                cross[first] += product[:GROUP, :GROUP]
+                cross[first + 1] += product[GROUP:, GROUP:]
+            return carry
+
+        lax.fori_loop(0, GROUPS * GROUP // ROWS, transform, 0)
+
+    def pair(p, carry):
+        center(2 * p, 0)
+        center(2 * p + 1, 1)
+        accumulate(2 * cols)
+        return carry
+
+    lax.fori_loop(0, chunks // 2 - 1, pair, 0)
+
+    def single(s, carry):
+        center(s, 0)
+        accumulate(cols)
+        return carry
+
+    lax.fori_loop(chunks - 2, chunks, single, 0)
 
     band_mask = mask[...].astype(jnp.bfloat16)
     same_bin = (
@@ -301,7 +318,7 @@
         out_specs=pl.BlockSpec(memory_space=pltpu.VMEM),
         scratch_shapes=[
             pltpu.VMEM((chunks, frame_total, cols), jnp.bfloat16),
-            pltpu.VMEM((frame_total, cols), jnp.bfloat16),
+            pltpu.VMEM((frame_total, 2 * cols), jnp.bfloat16),
             pltpu.VMEM((GROUPS * GROUP, frame_total), jnp.bfloat16),
             pltpu.VMEM((GROUPS, GROUP, GROUP), jnp.float32),
             pltpu.VMEM(trig.shape, jnp.float32),

time: 213 us -> 211 us (level)
  no operation moved by 1% of the time
where the time goes in v3:
time: 211 us; the launch traced here: 210 us
  Pallas kernels  209 us (99%)
    pallas_call x1, Pallas kernels, local(): pl.pallas_call(functools.partial(kernel, groups, pixes, float(pix_dev * p...  209 us

profile of v3, /device:TPU:0, one launch (start us, length us, event | category | flops | bytes accessed | tf_op | source)
XLA Modules:
  0.0 210.5 jit_solution(391007332406147074)
XLA Ops:
  0.0 209.1 %band_coherence.1 = f32[8,128]{1,0:T(8,128)} custom-call(s32[65]{0:T(128)} %edges_ref.1, bf16[128,32768]{1,0:T(8,128)(2,1)} %frames_ref.1, f32[768,1024]{1,0:T(8,128)} %constant.8.clone.trig_hbm, f32[8,1024]{1,0:T(8,128)} %constant.9.clone.tapers_hbm, bf16[2048,128]{1,0:T(8,128)(2,1)} %constant.10.clone.combine_hbm, f32[128,256]{1,0:T(8,128)} %constant.11.clone.power_hbm), custom_call_target="tpu_custom_call" | custom-call | flops 51539607552 | bytes 16777216 | tf_op jit(solution)/shard_map/band_coherence/pallas_call | solution.py:314
  209.1 1.4 reshape.3

commit v4 on v3

--- a/solution.py
+++ b/solution.py
@@ -16,7 +16,7 @@
 PAIRS = TAPERS * TAPERS
 BINS = 8
 TILE = 256
-CHUNK = 256
+CHUNK = 512
 GROUP = 2 * TAPERS * BINS
 GROUPS = NB // BINS
 ROWS = 2048
@@ -64,6 +64,8 @@
     chunks, frame_total, cols = data.shape
     frames_dev = frame_total // groups
     share_cols = chunks * cols
+    last = chunks - 1
+    narrow = cols // 2
     own_bands = NBANDS // groups
     tiles = frame_total // TILE
     half = groups // 2
@@ -82,8 +84,22 @@
     def rows_of(group):
         return pl.ds(pl.multiple_of(group * frames_dev, frames_dev), frames_dev)
 
-    def columns_of(group, s):
-        return pl.ds(pl.multiple_of(group * share_cols + s * cols, 128), cols)
+    def columns_of(group, piece):
+        block, side = piece
+        start = group * share_cols + block * cols
+        if side is None:
+            return pl.ds(pl.multiple_of(start, 128), cols)
+        return pl.ds(pl.multiple_of(start + side * narrow, 128), narrow)
+
+    def place_of(group, piece):
+        block, side = piece
+        if side is None:
+            return data.at[block, rows_of(group), :]
+        return data.at[block, rows_of(group), side * narrow:(side + 1) * narrow]
+
+    def slot_of(piece):
+        block, side = piece
+        return block if side is None else last + side
 
     barrier = pltpu.get_barrier_semaphore()
     for d in peers:
@@ -96,38 +112,35 @@
         )
     pl.semaphore_wait(barrier, groups - 1 + pixes - 1)
 
-    def frame_copy(s, d):
+    def frame_copy(piece, d):
         to = target_of(d)
         return pltpu.make_async_remote_copy(
-            src_ref=frames_ref.at[:, columns_of(to, s)],
-            dst_ref=data.at[s, rows_of(me), :],
-            send_sem=send_sem.at[s, d],
-            recv_sem=recv_sem.at[s, d],
+            src_ref=frames_ref.at[:, columns_of(to, piece)],
+            dst_ref=place_of(me, piece),
+            send_sem=send_sem.at[slot_of(piece), d],
+            recv_sem=recv_sem.at[slot_of(piece), d],
             device_id=(to, me_pix),
             device_id_type=MESH,
         )
 
-    def own_copy(s):
+    def own_copy(piece):
         return pltpu.make_async_copy(
-            frames_ref.at[:, columns_of(me, s)], data.at[s, rows_of(me), :], local_sem.at[s]
-        )
-
-    def send(s, carry):
-        for d in across:
-            frame_copy(s, d).start()
-        for near in (2 * s, 2 * s + 1):
-            for d in beside:
-                frame_copy(near, d).start()
-            own_copy(near).start()
+            frames_ref.at[:, columns_of(me, piece)], place_of(me, piece),
+            local_sem.at[slot_of(piece)],
+        )
+
+    def send(piece):
+        for d in peers:
+            frame_copy(piece, d).start()
+        own_copy(piece).start()
+
+    def send_block(s, carry):
+        send((s, None))
         return carry
 
-    def send_across(s, carry):
-        for d in across:
-            frame_copy(s, d).start()
-        return carry
-
-    lax.fori_loop(0, chunks // 2, send, 0)
-    lax.fori_loop(chunks // 2, chunks, send_across, 0)
+    lax.fori_loop(0, last, send_block, 0)
+    for side in range(2):
+        send((last, side))
 
     table_copies = [
         pltpu.make_async_copy(source, target, table_sem.at[i])
@@ -159,27 +172,29 @@
 
     lax.fori_loop(0, GROUPS, fill, 0)
 
-    def center(s, slot):
-        own_copy(s).wait()
+    def center(piece):
+        block, side = piece
+        lanes = slice(0, cols) if side is None else slice(side * narrow, (side + 1) * narrow)
+        width = cols if side is None else narrow
+        own_copy(piece).wait()
         for d in peers:
             source = source_of(d)
             pltpu.make_async_remote_copy(
-                src_ref=frames_ref.at[:, columns_of(me, s)],
-                dst_ref=data.at[s, rows_of(source), :],
-                send_sem=send_sem.at[s, d],
-                recv_sem=recv_sem.at[s, d],
+                src_ref=frames_ref.at[:, columns_of(me, piece)],
+                dst_ref=place_of(source, piece),
+                send_sem=send_sem.at[slot_of(piece), d],
+                recv_sem=recv_sem.at[slot_of(piece), d],
                 device_id=(source, me_pix),
                 device_id_type=MESH,
             ).wait_recv()
-        total = jnp.zeros((1, cols), jnp.float32)
+        total = jnp.zeros((1, width), jnp.float32)
         for i in range(tiles):
-            block = data[s, i * TILE:(i + 1) * TILE, :].astype(jnp.float32)
-            total = total + jnp.sum(block, axis=0, keepdims=True)
+            values = data[block, i * TILE:(i + 1) * TILE, lanes].astype(jnp.float32)
+            total = total + jnp.sum(values, axis=0, keepdims=True)
         mean = total * (1.0 / frame_total)
         for i in range(tiles):
-            block = data[s, i * TILE:(i + 1) * TILE, :].astype(jnp.float32)
-            block = (block - mean).astype(jnp.bfloat16)
-            centered[i * TILE:(i + 1) * TILE, slot * cols:(slot + 1) * cols] = block
+            values = data[block, i * TILE:(i + 1) * TILE, lanes].astype(jnp.float32)
+            centered[i * TILE:(i + 1) * TILE, :width] = (values - mean).astype(jnp.bfloat16)
 
     def accumulate(width):
         def transform(r, carry):
@@ -199,20 +214,15 @@
 
         lax.fori_loop(0, GROUPS * GROUP // ROWS, transform, 0)
 
-    def pair(p, carry):
-        center(2 * p, 0)
-        center(2 * p + 1, 1)
-        accumulate(2 * cols)
-        return carry
-
-    lax.fori_loop(0, chunks // 2 - 1, pair, 0)
-
-    def single(s, carry):
-        center(s, 0)
+    def whole_block(s, carry):
+        center((s, None))
         accumulate(cols)
         return carry
 
-    lax.fori_loop(chunks - 2, chunks, single, 0)
+    lax.fori_loop(0, last, whole_block, 0)
+    for side in range(2):
+        center((last, side))
+        accumulate(narrow)
 
     band_mask = mask[...].astype(jnp.bfloat16)
     same_bin = (
@@ -225,11 +235,8 @@
         for row in (a, a + 1):
             side = jnp.where(same_bin[None], cross[:, row * BINS:(row + 1) * BINS, :], 0.0)
             sides.append(side.reshape(NB, GROUP))
-        high, low = split(jnp.concatenate(sides, axis=1))
-        pieces.append(
-            jnp.dot(band_mask, high, preferred_element_type=jnp.float32)
-            + jnp.dot(band_mask, low, preferred_element_type=jnp.float32)
-        )
+        sides = jnp.concatenate(sides, axis=1).astype(jnp.bfloat16)
+        pieces.append(jnp.dot(band_mask, sides, preferred_element_type=jnp.float32))
     high, low = split(jnp.concatenate(pieces, axis=1))
     both = jnp.dot(
         jnp.concatenate([high, low], axis=0), combine[...], preferred_element_type=jnp.float32
@@ -289,10 +296,13 @@
 
     def drain(s, carry):
         for d in peers:
-            frame_copy(s, d).wait_send()
+            frame_copy((s, None), d).wait_send()
         return carry
 
-    lax.fori_loop(0, chunks, drain, 0)
+    lax.fori_loop(0, last, drain, 0)
+    for side in range(2):
+        for d in peers:
+            frame_copy((last, side), d).wait_send()
     for d in peers:
         band_copy(d, target_of(d), me).wait_send()
     for d in range(1, pixes):
@@ -318,7 +328,7 @@
         out_specs=pl.BlockSpec(memory_space=pltpu.VMEM),
         scratch_shapes=[
             pltpu.VMEM((chunks, frame_total, cols), jnp.bfloat16),
-            pltpu.VMEM((frame_total, 2 * cols), jnp.bfloat16),
+            pltpu.VMEM((frame_total, cols), jnp.bfloat16),
             pltpu.VMEM((GROUPS * GROUP, frame_total), jnp.bfloat16),
             pltpu.VMEM((GROUPS, GROUP, GROUP), jnp.float32),
             pltpu.VMEM(trig.shape, jnp.float32),
@@ -332,9 +342,9 @@
             pltpu.VMEM((own_bands, lanes), jnp.float32),
             pltpu.VMEM((pixes, own_bands, lanes), jnp.float32),
             pltpu.SemaphoreType.DMA((4,)),
-            pltpu.SemaphoreType.DMA((chunks,)),
-            pltpu.SemaphoreType.DMA((chunks, groups)),
-            pltpu.SemaphoreType.DMA((chunks, groups)),
+            pltpu.SemaphoreType.DMA((chunks + 1,)),
+            pltpu.SemaphoreType.DMA((chunks + 1, groups)),
+            pltpu.SemaphoreType.DMA((chunks + 1, groups)),
             pltpu.SemaphoreType.DMA((groups,)),
             pltpu.SemaphoreType.DMA((groups,)),
             pltpu.SemaphoreType.DMA((pixes,)),

time: 211 us -> 212 us (level)
  no operation moved by 1% of the time
where the time goes in v4:
time: 212 us; the launch traced here: 211 us
  Pallas kernels  210 us (99%)
    pallas_call x1, Pallas kernels, local(): pl.pallas_call(functools.partial(kernel, groups, pixes, float(pix_dev * p...  210 us

profile of v4, /device:TPU:0, one launch (start us, length us, event | category | flops | bytes accessed | tf_op | source)
XLA Modules:
  0.0 211.3 jit_solution(1513967446337414351)
XLA Ops:
  0.0 209.9 %band_coherence.1 = f32[8,128]{1,0:T(8,128)} custom-call(s32[65]{0:T(128)} %edges_ref.1, bf16[128,32768]{1,0:T(8,128)(2,1)} %frames_ref.1, f32[768,1024]{1,0:T(8,128)} %constant.8.clone.trig_hbm, f32[8,1024]{1,0:T(8,128)} %constant.9.clone.tapers_hbm, bf16[2048,128]{1,0:T(8,128)(2,1)} %constant.10.clone.combine_hbm, f32[128,256]{1,0:T(8,128)} %constant.11.clone.power_hbm), custom_call_target="tpu_custom_call" | custom-call | flops 51539607552 | bytes 16777216 | tf_op jit(solution)/shard_map/band_coherence/pallas_call | solution.py:324
  209.9 1.4 reshape.3

commit v5 on v4

--- a/solution.py
+++ b/solution.py
@@ -17,6 +17,7 @@
 BINS = 8
 TILE = 256
 CHUNK = 512
+WINDOW = 2
 GROUP = 2 * TAPERS * BINS
 GROUPS = NB // BINS
 ROWS = 2048
@@ -138,9 +139,14 @@
         send((s, None))
         return carry
 
-    lax.fori_loop(0, last, send_block, 0)
-    for side in range(2):
-        send((last, side))
+    def send_halves():
+        for side in range(2):
+            send((last, side))
+
+    ahead = min(WINDOW, last)
+    lax.fori_loop(0, ahead, send_block, 0)
+    if last == 0:
+        send_halves()
 
     table_copies = [
         pltpu.make_async_copy(source, target, table_sem.at[i])
@@ -216,10 +222,18 @@
 
     def whole_block(s, carry):
         center((s, None))
+        if carry is None:
+            send_halves()
+        elif carry is not False:
+            send_block(s + ahead, carry)
         accumulate(cols)
         return carry
 
-    lax.fori_loop(0, last, whole_block, 0)
+    if last > 0:
+        lax.fori_loop(0, last - ahead, whole_block, 0)
+        whole_block(last - ahead, None)
+        for s in range(last - ahead + 1, last):
+            whole_block(s, False)
     for side in range(2):
         center((last, side))
         accumulate(narrow)

time: 212 us -> 211 us (level)
  no operation moved by 1% of the time
where the time goes in v5:
time: 211 us; the launch traced here: 210 us
  Pallas kernels  209 us (99%)
    pallas_call x1, Pallas kernels, local(): pl.pallas_call(functools.partial(kernel, groups, pixes, float(pix_dev * p...  209 us

profile of v5, /device:TPU:0, one launch (start us, length us, event | category | flops | bytes accessed | tf_op | source)
XLA Modules:
  0.0 210.4 jit_solution(1414244177124273257)
XLA Ops:
  0.0 209.0 %band_coherence.1 = f32[8,128]{1,0:T(8,128)} custom-call(s32[65]{0:T(128)} %edges_ref.1, bf16[128,32768]{1,0:T(8,128)(2,1)} %frames_ref.1, f32[768,1024]{1,0:T(8,128)} %constant.8.clone.trig_hbm, f32[8,1024]{1,0:T(8,128)} %constant.9.clone.tapers_hbm, bf16[2048,128]{1,0:T(8,128)(2,1)} %constant.10.clone.combine_hbm, f32[128,256]{1,0:T(8,128)} %constant.11.clone.power_hbm), custom_call_target="tpu_custom_call" | custom-call | flops 51539607552 | bytes 16777216 | tf_op jit(solution)/shard_map/band_coherence/pallas_call | solution.py:338
  209.0 1.4 reshape.3
